TPU v7x, 32 devices: a whole 2x2x4 slice. The times are simulated.
32 devices in a mesh: groups: 2 (over y), clus: 4 (over x, core), help: 4 (over z).
Axes of the slice: x: 2, y: 2, z: 4, core: 2. Of those that a mesh axis runs over, the one named last changes fastest.
Arguments:
- item_row_blocks: bfloat16 [512, 128, 1024], P(('groups', 'clus', 'help')), parts along dimension 0, may hold values from -4 to 4
- block_cluster: int32 [512, 1], P(('groups', 'clus', 'help')), parts along dimension 0, may hold values from 0 to 3; in each aligned block of 16 rows (0 to 15, 16 to 31, ...) at most 8 rows name the same one
- cluster_owner: int32 [8], P('groups'), parts along dimension 0, may hold values from 0 to 3, each once
- query_rows: bfloat16 [8, 1024, 1024], P(('groups', 'clus'), 'help'), parts along dimension 0, may hold values from -0.125 to 0.125
- sketch_rows: bfloat16 [8, 32, 1024], P(('groups', 'clus'), None, 'help'), parts along dimension 0, may hold values from -0.125 to 0.125
Outputs:
- query_basis: float32 [8, 32, 1024], P(('groups', 'clus'), None, 'help'), parts along dimension 0
- item_codes: bfloat16 [512, 32, 128], P(('groups', 'clus', 'help')), parts along dimension 0
There are 2 independent parts, one for each index of `groups`. A program takes and returns all parts, laid end to end along the dimension named above; each array names one. Nothing has to cross between parts.
Inputs may be any that keep to these rules, and one draw needn't show every extreme that they name: `block_cluster`: among the 16 blocks stored on one device at most 8 belong to one cluster, and on some devices one cluster has exactly 8; every cluster has a block somewhere. A permutation: the queries, sketch and basis of cluster k stand at index cluster_owner[k].
All inputs are finite; a program needn't handle non-finite values.
Results may differ from a plain program's by a relative error of at most 0.0051.
Values may be sent and summed in bfloat16 or wider, within the bound.
A program may use at most 64 MiB of HBM per device.

v0:
```python
import jax
import jax.numpy as jnp
from jax import lax
from jax.sharding import PartitionSpec as P

POWER = 2


def place_blocks(block_cluster, cluster_owner, slot_count, capacity):
    cluster_ids = block_cluster[:, 0]
    each_cluster_list = jnp.arange(cluster_owner.shape[0], dtype=jnp.int32)
    owner_row = jnp.sum(
        jnp.where(cluster_ids[:, None] == each_cluster_list[None, :], cluster_owner[None, :], 0),
        axis=1,
    )
    stored = cluster_ids.shape[0]
    order_ids = jnp.arange(stored, dtype=jnp.int32)
    same_owner = owner_row[:, None] == owner_row[None, :]
    earlier = order_ids[None, :] < order_ids[:, None]
    position = jnp.sum(jnp.where(same_owner & earlier, 1, 0), axis=1)
    slot_index = owner_row * capacity + position
    slot_ids = jnp.arange(slot_count, dtype=jnp.int32)
    return (slot_ids[:, None] == slot_index[None, :]).astype(jnp.bfloat16)


def orthonormal(summed):
    gram_matrix = jnp.dot(
        summed, summed.T, precision=lax.Precision.HIGHEST, preferred_element_type=jnp.float32
    )
    factor_lower = jnp.linalg.cholesky(gram_matrix)
    return lax.linalg.triangular_solve(factor_lower, summed, left_side=True, lower=True)


def on_device(item_row_blocks, block_cluster, cluster_owner, query_rows, sketch_rows):
    clus_count = lax.axis_size("clus")
    stored = item_row_blocks.shape[0]
    block_rows = item_row_blocks.shape[1]
    depth = item_row_blocks.shape[2]
    capacity = 2 * stored // clus_count
    slot_count = clus_count * capacity
    share_width = query_rows.shape[1]
    indicator_matrix = place_blocks(block_cluster, cluster_owner, slot_count, capacity)
    packed = jnp.einsum(
        "vl,lap->vap", indicator_matrix, item_row_blocks, preferred_element_type=jnp.float32
    ).astype(jnp.bfloat16)
    packed = packed.reshape(clus_count, capacity, block_rows, depth)
    all_queries, complete_sketch = (
        lax.all_gather(query_rows, "help", axis=1, tiled=True),
        lax.all_gather(sketch_rows, "help", axis=2, tiled=True),
    )
    full_queries = all_queries[0]
    entire_sketch = complete_sketch[0]
    arrived = lax.all_to_all(packed, "clus", split_axis=0, concat_axis=0, tiled=True)
    raw = jnp.einsum("md,nckd->ncmk", full_queries, arrived, preferred_element_type=jnp.float32)
    scores = jnp.tanh(raw).astype(jnp.bfloat16)
    scores = scores.reshape(slot_count, full_queries.shape[0], block_rows)
    codes_now = jnp.einsum(
        "rm,smk->srk", entire_sketch, scores, preferred_element_type=jnp.float32
    ).astype(jnp.bfloat16)
    basis_share = jnp.zeros((sketch_rows.shape[1], share_width), jnp.float32)
    for power_step in range(POWER):
        partial_value = jnp.einsum(
            "srk,smk->rm", codes_now, scores, preferred_element_type=jnp.float32
        )
        summed = lax.psum(partial_value, "help")
        new_basis = orthonormal(summed)
        rounded = new_basis.astype(jnp.bfloat16)
        basis_share = lax.dynamic_slice_in_dim(
            new_basis, lax.axis_index("help") * share_width, share_width, 1
        )
        codes_now = jnp.einsum(
            "rm,smk->srk", rounded, scores, preferred_element_type=jnp.float32
        ).astype(jnp.bfloat16)
    returned = lax.all_to_all(
        codes_now.reshape(clus_count, capacity, codes_now.shape[1], block_rows),
        "clus",
        split_axis=0,
        concat_axis=0,
        tiled=True,
    )
    returned = returned.reshape(slot_count, codes_now.shape[1], block_rows)
    own_codes = jnp.einsum(
        "sb,srk->brk", indicator_matrix, returned, preferred_element_type=jnp.float32
    ).astype(jnp.bfloat16)
    return (basis_share[None], own_codes)


def solution(mesh):
    in_specs = (
        P(("groups", "clus", "help"), None, None),
        P(("groups", "clus", "help"), None),
        P("groups"),
        P(("groups", "clus"), "help", None),
        P(("groups", "clus"), None, "help"),
    )
    out_specs = (P(("groups", "clus"), None, "help"), P(("groups", "clus", "help"), None, None))
    return jax.shard_map(
        on_device, mesh=mesh, in_specs=in_specs, out_specs=out_specs, check_vma=False
    )
```

profile of v0, /device:TPU:0, one launch (start us, length us, event | category | flops | bytes accessed | tf_op | source)
XLA Modules:
  0.0 275.8 jit_solution(3309670487409732223)
XLA Ops:
  7.2 0.8 select_reduce_fusion.2
  8.1 8.8 %convert_bitcast_fusion = bf16[4,8,128,1024]{3,1,0,2:T(8,128)(2,1)} fusion(bf16[16,128,1024]{2,1,0:T(8,128)(2,1)} %param.8, s32[16]{0:T(128)S(1)} %multiply_add_fusion), kind=kOutput, calls=%fused_computation.1 | convolution fusion | flops 138412544 | bytes 12582976 | tf_op jit(solution)/shard_map/vl,lap->vap/dot_general | solution.py:43
  16.9 11.4 %copy.17 = bf16[4,8,128,1024]{3,2,1,0:T(8,128)(2,1)} copy(bf16[4,8,128,1024]{3,1,0,2:T(8,128)(2,1)} %convert_bitcast_fusion) | data formatting | bytes 16777216 | tf_op jit(solution)/shard_map/reshape | solution.py:46
  28.2 5.8 %all-to-all-start = ((bf16[4,8,128,1024]{3,2,1,0:T(8,128)(2,1)}), bf16[4,8,128,1024]{3,2,1,0:T(8,128)(2,1)}, u32[]{:S(2)}, u32[]{:S(2)}) async-start(bf16[4,8,128,1024]{3,2,1,0:T(8,128)(2,1)} %copy.17), calls=%async_computation | async-start | bytes 16777216 | tf_op jit(solution)/shard_map/all_to_all | solution.py:53
  34.1 0.7 all-gather.2.cloned.1.call-update
  34.9 15.0 %all_gather.7 = bf16[1,32,1024]{2,1,0:T(8,128)(2,1)S(1)} all-gather(bf16[1,32,256]{2,1,0:T(8,128)(2,1)S(1)} %copy-done), channel_id=1, replica_groups=mesh['groups'=2,'clus'=4,'help'=4] {'help'}, dimensions={2}, use_global_device_ids=true | all-gather | bytes 81920 | tf_op jit(solution)/shard_map/all_gather | solution.py:49
  49.8 35.8 %all-gather.2.cloned.1.call-done = bf16[1,1024,1024]{2,1,0:T(8,128)(2,1)} async-done(((bf16[1,256,1024]{2,1,0:T(8,128)(2,1)}), bf16[1,1024,1024]{2,1,0:T(8,128)(2,1)}) %all-gather.2.cloned.1.call-update) | async-done | bytes 2097168 | tf_op jit(solution)/shard_map/all_gather | solution.py:48
  85.6 42.2 %all-to-all-done = bf16[4,8,128,1024]{3,2,1,0:T(8,128)(2,1)} async-done(((bf16[4,8,128,1024]{3,2,1,0:T(8,128)(2,1)}), bf16[4,8,128,1024]{3,2,1,0:T(8,128)(2,1)}, u32[]{:S(2)}, u32[]{:S(2)}) %all-to-all-start) | async-done | bytes 8388640 | tf_op jit(solution)/shard_map/all_to_all | solution.py:53
  127.8 15.0 %tanh_convert_fusion = bf16[4,8,128,1024]{3,2,1,0:T(8,128)(2,1)} fusion(bf16[4,8,128,1024]{3,2,1,0:T(8,128)(2,1)} %all-to-all-done, bf16[1,1024,1024]{2,1,0:T(8,128)(2,1)} %all-gather.2.cloned.1.call-done), kind=kOutput, calls=%fused_computation | convolution fusion | flops 8594128896 | bytes 18874368 | tf_op jit(solution)/shard_map/md,nckd->ncmk/dot_general | solution.py:54
  142.7 10.4 %fusion.7 = f32[32,1024]{1,0:T(8,128)} fusion(bf16[32,1024,128]{1,2,0:T(8,128)(2,1)} %bitcast.82, bf16[1,32,1024]{2,1,0:T(8,128)(2,1)S(1)} %all_gather.7), kind=kOutput, calls=%fused_computation.13 | convolution fusion | flops 537001984 | bytes 8585216 | tf_op jit(solution)/shard_map/srk,smk->rm/dot_general | solution.py:62
  153.2 0.3 all-reduce.5.cloned.1.call-start
  153.4 35.5 %all-reduce.3.cloned.1.call-done = f32[32,1024]{1,0:T(8,128)} async-done(((f32[32,1024]{1,0:T(8,128)}), f32[32,1024]{1,0:T(8,128)}) %all-reduce.3.cloned.1.call-update) | async-done | bytes 131088 | tf_op jit(solution)/shard_map/psum | solution.py:65
  189.0 1.2 fusion.30
  190.3 2.9 %cholesky.44 = f32[32,32]{1,0:T(8,128)S(1)} custom-call(f32[32,32]{1,0:T(8,128)S(1)} %fusion.21), custom_call_target="Cholesky" | custom-call | tf_op jit(solution)/shard_map/jit(cholesky)/cholesky | solution.py:30
  193.3 0.6 compare_reduce_fusion.1
  193.9 0.7 fusion.15
  194.6 2.4 custom-call.6
  197.0 1.2 fusion.8
  198.2 10.4 %fusion.6 = f32[32,1024]{1,0:T(8,128)} fusion(bf16[32,1024,128]{1,2,0:T(8,128)(2,1)} %bitcast.83, bf16[32,1024,1]{1,0,2:T(8,128)(2,1)S(1)} %fusion.8), kind=kOutput, calls=%fused_computation.12 | convolution fusion | flops 537001984 | bytes 8585216 | tf_op jit(solution)/shard_map/srk,smk->rm/dot_general | solution.py:62
  208.7 34.3 %all-reduce.5.cloned.1.call-done = f32[32,1024]{1,0:T(8,128)} async-done(((f32[32,1024]{1,0:T(8,128)}), f32[32,1024]{1,0:T(8,128)}) %all-reduce.5.cloned.1.call-update) | async-done | bytes 131088 | tf_op jit(solution)/shard_map/psum | solution.py:65
  243.0 1.2 fusion.31
  244.3 2.9 %cholesky.55 = f32[32,32]{1,0:T(8,128)S(1)} custom-call(f32[32,32]{1,0:T(8,128)S(1)} %fusion.19), custom_call_target="Cholesky" | custom-call | tf_op jit(solution)/shard_map/jit(cholesky)/cholesky | solution.py:30
  247.3 0.6 compare_reduce_fusion
  247.9 0.7 fusion.16
  248.6 2.4 custom-call.7
  251.0 1.2 fusion.17
  252.3 6.7 %convolution_convert_fusion = bf16[32,128,32]{1,2,0:T(8,128)(2,1)} fusion(bf16[32,1024,128]{1,2,0:T(8,128)(2,1)} %bitcast.84, f32[32,1024]{1,0:T(8,128)S(1)} %fusion.17), kind=kOutput, calls=%fused_computation.4 | convolution fusion | flops 268599296 | bytes 8781824 | tf_op jit(solution)/shard_map/rm,smk->srk/dot_general | solution.py:71
  258.9 3.4 %all-to-all-start.1 = ((bf16[4,8,32,128]{3,2,1,0:T(8,128)(2,1)}), bf16[4,8,32,128]{3,2,1,0:T(8,128)(2,1)S(1)}, u32[]{:S(2)}, u32[]{:S(2)}) async-start(bf16[4,8,32,128]{3,2,1,0:T(8,128)(2,1)} %bitcast.25), calls=%async_computation.1 | async-start | bytes 524288 | tf_op jit(solution)/shard_map/all_to_all | solution.py:74
  262.3 0.6 dynamic-slice_bitcast_fusion
  262.9 5.4 %all-to-all-done.1 = bf16[4,8,32,128]{3,2,1,0:T(8,128)(2,1)S(1)} async-done(((bf16[4,8,32,128]{3,2,1,0:T(8,128)(2,1)}), bf16[4,8,32,128]{3,2,1,0:T(8,128)(2,1)S(1)}, u32[]{:S(2)}, u32[]{:S(2)}) %all-to-all-start.1) | async-done | bytes 262176 | tf_op jit(solution)/shard_map/all_to_all | solution.py:74
  268.3 0.2 convolution_convert_fusion.3
  268.6 0.7 copy.24
  (14 shorter events, 0.5 us)
Async XLA Ops:
  28.2 6.6 %copy-start = (bf16[1,32,256]{2,1,0:T(8,128)(2,1)S(1)}, bf16[1,32,256]{2,1,0:T(8,128)(2,1)}, u32[]{:S(2)}) copy-start(bf16[1,32,256]{2,1,0:T(8,128)(2,1)} %param.12) | copy-start | bytes 49156
  28.2 99.5 %all-to-all-start = ((bf16[4,8,128,1024]{3,2,1,0:T(8,128)(2,1)}), bf16[4,8,128,1024]{3,2,1,0:T(8,128)(2,1)}, u32[]{:S(2)}, u32[]{:S(2)}) async-start(bf16[4,8,128,1024]{3,2,1,0:T(8,128)(2,1)} %copy.17), calls=%async_computation | async-start | bytes 16777216 | tf_op jit(solution)/shard_map/all_to_all | solution.py:53
  34.1 51.5 %all-gather.2.cloned.1.call-start = ((), (), s32[]{:S(2)}) async-start(), calls=%async_computation.2 | async-start | bytes 2621440 | tf_op jit(solution)/shard_map/all_gather | solution.py:48
  34.8 154.2 %all-reduce.3.cloned.1.call-start = ((), (), s32[]{:S(2)}) async-start(), calls=%async_computation.3 | async-start | bytes 262144 | tf_op jit(solution)/shard_map/psum | solution.py:65
  153.2 89.8 %all-reduce.5.cloned.1.call-start = ((), (), s32[]{:S(2)}) async-start(), calls=%async_computation.4 | async-start | bytes 262144 | tf_op jit(solution)/shard_map/psum | solution.py:65
  258.9 9.4 %all-to-all-start.1 = ((bf16[4,8,32,128]{3,2,1,0:T(8,128)(2,1)}), bf16[4,8,32,128]{3,2,1,0:T(8,128)(2,1)S(1)}, u32[]{:S(2)}, u32[]{:S(2)}) async-start(bf16[4,8,32,128]{3,2,1,0:T(8,128)(2,1)} %bitcast.25), calls=%async_computation.1 | async-start | bytes 524288 | tf_op jit(solution)/shard_map/all_to_all | solution.py:74
Sparse Core Ops, SparseCore 0:
  36.5 49.0 all-gather.1
  153.3 35.6 all-reduce.2
  208.8 34.1 all-reduce.4
where the time goes:
time: 276 us
  waiting for transfers between devices  154 us (56%)
  matrix products  56.4 us (20%)
  blocking collectives  15 us (5%)
  other arithmetic  14.3 us (5%)
  between operations  13.8 us (5%)
  local copies, waits for them, and re-layouts  12.8 us (5%)
  starting transfers between devices  9.57 us (3%)
    psum x2, waiting for transfers between devices, on_device(): summed = lax.psum(partial_value, 'help')  69.8 us
    all_to_all x1, waiting for transfers between devices, on_device(): lax.all_to_all(packed, 'clus', split_axis=0, concat_axis=0, tiled=True)  42.2 us
    all_gather x1, waiting for transfers between devices, on_device(): lax.all_gather(query_rows, 'help', axis=1, tiled=True)  35.8 us
    dot_general x2, matrix products, on_device(): jnp.einsum('srk,smk->rm', codes_now, scores, preferred_element_type=jnp.f...  20.9 us
    all_gather x1, blocking collectives, on_device(): lax.all_gather(sketch_rows, 'help', axis=2, tiled=True)  15 us
    dot_general x1, matrix products, on_device(): jnp.einsum('md,nckd->ncmk', full_queries, arrived, preferred_element_type...  15 us
    reshape x1, local copies, waits for them, and re-layouts, on_device(): packed = packed.reshape(clus_count, capacity, block_rows, depth)  11.4 us
    dot_general x1, matrix products, on_device(): jnp.einsum('vl,lap->vap', indicator_matrix, item_row_blocks, preferred_el...  8.75 us
  transfers between devices with their start and end apart: 5, of which 5 were waited for; matrix products, arithmetic and copies ran while one was open for 0% of the time, Pallas kernels for 0%

commit v1 on v0

v1 whole, which is shorter than its diff:
```python
import functools

import jax
import jax.numpy as jnp
from jax import lax
from jax.experimental import pallas as pl
from jax.experimental.pallas import tpu as pltpu
from jax.sharding import PartitionSpec as P

POWER = 2
CORES = 2
MESH = pl.DeviceIdType.MESH
F32 = jnp.float32
BF16 = jnp.bfloat16
NT = (((1,), (1,)), ((), ()))


def dot_nt(a, b, precision=None):
    return lax.dot_general(a, b, NT, precision=precision, preferred_element_type=F32)


def invert_factor(gram):
    rank = gram.shape[0]
    row = lax.broadcasted_iota(jnp.int32, gram.shape, 0)
    lane = lax.broadcasted_iota(jnp.int32, gram.shape, 1)
    work = jnp.where(lane == row + rank, 1.0, gram)
    row1 = lax.broadcasted_iota(jnp.int32, (rank, 1), 0)
    scale = jnp.zeros((rank, 1), F32)
    for k in range(rank):
        pivot_row = work[k : k + 1, :]
        column = work[:, k : k + 1]
        pivot = pivot_row[:, k : k + 1]
        scale = jnp.where(row1 == k, lax.rsqrt(pivot), scale)
        factor = jnp.where(row1 > k, column / pivot, 0.0)
        work = work - factor * pivot_row
    return (work * scale)[:, rank : 2 * rank]


def kernel(
    clus, help_, cap,
    src_ref, slot_ref, owner_ref, item_ref, query_ref, sketch_ref,
    basis_ref, codes_ref,
    queries, items, packed, slots, left, partial, from_clus, total, from_help, grams,
    load_sem, zs, zr, xs, xr, cs, cr, gzs, gzr, gxs, gxr, as_, ar, bs, br, ms, mr,
):
    nx = clus // CORES
    stored, block_rows, depth = items.shape
    share = query_ref.shape[0]
    rank = sketch_ref.shape[0]
    c = lax.axis_index("clus")
    h = lax.axis_index("help")
    x = c // CORES
    core = c % CORES
    sib = x * CORES + (1 - core)

    def at(ci, hi):
        return {"clus": ci, "help": hi}

    load_query = pltpu.make_async_copy(query_ref, queries.at[c * help_ + h], load_sem.at[0])
    load_items = pltpu.make_async_copy(item_ref, items, load_sem.at[1])
    own_rows = pl.ds(pl.multiple_of(c * rank, rank), rank)

    def cols(j):
        return pl.ds(pl.multiple_of(j * share, share), share)

    load_sketch = pltpu.make_async_copy(
        sketch_ref, left.at[0, own_rows, cols(h)], load_sem.at[2]
    )
    load_query.start()
    load_sketch.start()
    load_items.start()

    barrier = pltpu.get_barrier_semaphore()
    for k in range(1, clus):
        pl.semaphore_signal(
            barrier, inc=1, device_id=at(lax.rem(c + k, clus), h), device_id_type=MESH
        )
    for k in range(1, help_):
        pl.semaphore_signal(
            barrier, inc=1, device_id=at(c, lax.rem(h + k, help_)), device_id_type=MESH
        )
    pl.semaphore_wait(barrier, clus + help_ - 2)

    def remote(ref, send, recv, ci, hi):
        return pltpu.make_async_remote_copy(
            src_ref=ref, dst_ref=ref, send_sem=send, recv_sem=recv,
            device_id=at(ci, hi), device_id_type=MESH,
        )

    def z_copy(d, j):
        hi = jnp.clip(h + 1 if d == 0 else h - 1, 0, help_ - 1)
        return remote(queries.at[c * help_ + j], zs.at[d, j], zr.at[j], c, hi)

    def x_copy(ci, dx, j):
        other = lax.rem(x + dx, nx) * CORES + core
        return remote(queries.at[ci * help_ + j], xs.at[dx, j], xr.at[dx, j], other, h)

    def core_copy(ci, dx, j):
        return remote(queries.at[ci * help_ + j], cs.at[dx, j], cr.at[dx, j], sib, h)

    def slice_of(s, d):
        j = jnp.where(d == 0, h - s, h + s)
        ok = (j >= 0) & (j < help_) & (s >= 0) & ((s > 0) | (d == 0))
        return jnp.clip(j, 0, help_ - 1), ok

    def spread(s):
        for d in range(2):
            j, ok = slice_of(s, d)

            @pl.when(ok)
            def _():
                if not (isinstance(s, int) and s == 0):
                    z_copy(d, j).wait_recv()

                @pl.when(h < help_ - 1 if d == 0 else h > 0)
                def _():
                    z_copy(d, j).start()

                if isinstance(s, int) and s == 0 and d == 0:

                    @pl.when(h > 0)
                    def _():
                        z_copy(1, j).start()

                for dx in range(1, nx):
                    x_copy(c, dx, j).start()
                core_copy(c, 0, j).start()

    group_rows = min(4, cap)

    def score(ci, j):
        @pl.loop(0, cap // group_rows)
        def _(g):
            first = ci * cap + g * group_rows
            rows = packed[pl.ds(first, group_rows)].reshape(group_rows * block_rows, depth)
            raw = dot_nt(rows, queries[ci * help_ + j])
            slots[pl.ds(first, group_rows), :, cols(j)] = (
                jnp.tanh(raw).astype(BF16).reshape(group_rows, block_rows, share)
            )

    def gz(stage, k):
        return remote(
            left.at[stage, own_rows, cols(h)], gzs.at[stage, k], gzr.at[stage, k],
            c, lax.rem(h + k, help_),
        )

    def gx(stage, k):
        return remote(
            left.at[stage, own_rows], gxs.at[stage, k], gxr.at[stage, k],
            lax.rem(c + k, clus), h,
        )

    def gather_first(stage):
        for k in range(1, help_):
            gz(stage, k).start()

    def gather_second(stage):
        for k in range(1, help_):
            gz(stage, k).wait_recv()
        for k in range(1, clus):
            gx(stage, k).start()

    def gather_finish(stage):
        for k in range(1, clus):
            gx(stage, k).wait_recv()
        for k in range(1, help_):
            gz(stage, k).wait_send()
        for k in range(1, clus):
            gx(stage, k).wait_send()

    load_query.wait()
    spread(0)
    load_sketch.wait()
    gather_first(0)
    load_items.wait()

    @pl.loop(0, clus * cap)
    def _(s):
        packed[s] = items[src_ref[s]]

    gather_second(0)

    @pl.loop(0, help_ + 2)
    def _(s):
        @pl.when((s > 0) & (s < help_))
        def _():
            spread(s)

        @pl.loop(0, 2)
        def _(d):
            j, ok = slice_of(s, d)

            @pl.when(ok)
            def _():
                score(c, j)

        @pl.loop(0, 2)
        def _(d):
            j, ok = slice_of(s - 1, d)

            @pl.when(ok)
            def _():
                @pl.loop(1, nx)
                def _(dx):
                    ci = lax.rem(x + nx - dx, nx) * CORES + core
                    x_copy(ci, dx, j).wait_recv()
                    core_copy(ci, dx, j).start()

                core_copy(sib, 0, j).wait_recv()
                score(sib, j)

                @pl.loop(1, nx)
                def _(dx):
                    score(lax.rem(x + nx - dx, nx) * CORES + core, j)

        @pl.loop(0, 2)
        def _(d):
            j, ok = slice_of(s - 2, d)

            @pl.when(ok)
            def _():
                @pl.loop(1, nx)
                def _(dx):
                    ci = lax.rem(x + nx - dx, nx) * CORES + (1 - core)
                    core_copy(ci, dx, j).wait_recv()
                    score(ci, j)

    scores = items

    @pl.loop(0, stored)
    def _(b):
        scores[b] = slots[slot_ref[b]]

    group = 4
    width = group * block_rows
    row_owner = lax.broadcasted_iota(jnp.int32, (clus * rank, width), 0) // rank

    def make_codes(stage, g):
        part = scores[pl.ds(g * group, group)].reshape(width, left.shape[2])
        value = dot_nt(left[stage], part)
        keep = row_owner == owner_ref[g]
        return jnp.where(keep, value, 0.0), part

    def a_copy(it, k):
        to = lax.rem(c + k, clus)
        return pltpu.make_async_remote_copy(
            src_ref=partial.at[pl.ds(pl.multiple_of(to * rank, rank), rank)],
            dst_ref=from_clus.at[k],
            send_sem=as_.at[it, k], recv_sem=ar.at[it, k],
            device_id=at(to, h), device_id_type=MESH,
        )

    def b_copy(it, k):
        to = lax.rem(h + k, help_)
        return pltpu.make_async_remote_copy(
            src_ref=total.at[it, :, cols(to)],
            dst_ref=from_help.at[it, k],
            send_sem=bs.at[it, k], recv_sem=br.at[it, k],
            device_id=at(c, to), device_id_type=MESH,
        )

    def m_copy(it, k):
        return remote(grams.at[it, h], ms.at[it, k], mr.at[it, k], c, lax.rem(h + k, help_))

    gather_finish(0)
    for it in range(POWER):
        for g in range(stored // group):
            value, part = make_codes(it, g)
            term = jnp.dot(value.astype(BF16), part, preferred_element_type=F32)
            if g == 0:
                partial[...] = term
            else:
                partial[...] += term
        for k in range(1, clus):
            a_copy(it, k).start()
        summed = partial[own_rows]
        for k in range(1, clus):
            a_copy(it, k).wait_recv()
            summed = summed + from_clus[k]
        total[it] = summed
        for k in range(1, help_):
            b_copy(it, k).start()
        mine = total[it, :, cols(h)]
        for k in range(1, help_):
            b_copy(it, k).wait_recv()
            mine = mine + from_help[it, k]
        wide = jnp.concatenate([mine, jnp.zeros((128 - rank, share), F32)], axis=0)
        grams[it, h] = dot_nt(mine, wide, lax.Precision.HIGHEST)
        for k in range(1, help_):
            m_copy(it, k).start()
        for k in range(1, help_):
            m_copy(it, k).wait_recv()
        gram = grams[it, 0]
        for k in range(1, help_):
            gram = gram + grams[it, k]
        basis = jnp.dot(
            invert_factor(gram), mine,
            precision=lax.Precision.HIGHEST, preferred_element_type=F32,
        )
        left[it + 1, own_rows, cols(h)] = basis.astype(BF16)
        gather_first(it + 1)
        if it == POWER - 1:
            basis_ref[...] = basis
        gather_second(it + 1)
        for k in range(1, clus):
            a_copy(it, k).wait_send()
        for k in range(1, help_):
            b_copy(it, k).wait_send()
            m_copy(it, k).wait_send()
        gather_finish(it + 1)

    for g in range(stored // group):
        value, _ = make_codes(POWER, g)
        out = value[0:rank]
        for ci in range(1, clus):
            out = out + value[ci * rank : (ci + 1) * rank]
        out = out.astype(BF16)
        for b in range(group):
            codes_ref[g * group + b] = out[:, b * block_rows : (b + 1) * block_rows]

    @pl.loop(0, help_)
    def _(s):
        for d in range(2):
            j, ok = slice_of(s, d)

            @pl.when(ok)
            def _():
                @pl.when(h < help_ - 1 if d == 0 else h > 0)
                def _():
                    z_copy(d, j).wait_send()

                if d == 0:

                    @pl.when((s == 0) & (h > 0))
                    def _():
                        z_copy(1, j).wait_send()

                core_copy(c, 0, j).wait_send()
                for dx in range(1, nx):
                    x_copy(c, dx, j).wait_send()
                    core_copy(c, dx, j).wait_send()


def on_device(item_row_blocks, block_cluster, cluster_owner, query_rows, sketch_rows):
    clus = lax.axis_size("clus")
    help_ = lax.axis_size("help")
    stored, block_rows, depth = item_row_blocks.shape
    share = query_rows.shape[1]
    rank = sketch_rows.shape[1]
    queries_all = share * help_
    cap = 2 * stored // clus
    ids = block_cluster[:, 0]
    each = jnp.arange(clus, dtype=jnp.int32)
    owner = jnp.sum(jnp.where(ids[:, None] == each[None, :], cluster_owner[None, :], 0), axis=1)
    order = jnp.arange(stored, dtype=jnp.int32)
    earlier = (owner[:, None] == owner[None, :]) & (order[None, :] < order[:, None])
    slot = owner * cap + jnp.sum(earlier.astype(jnp.int32), axis=1)
    every_slot = jnp.arange(clus * cap, dtype=jnp.int32)
    source = jnp.sum(jnp.where(every_slot[:, None] == slot[None, :], order[None, :], 0), axis=1)
    owner_wide = jnp.repeat(owner, block_rows).reshape(stored // 4, 1, 4 * block_rows)

    nx = clus // CORES
    dma = pltpu.SemaphoreType.DMA
    smem = pl.BlockSpec(memory_space=pltpu.SMEM)
    vmem = pl.BlockSpec(memory_space=pltpu.VMEM)
    hbm = pl.BlockSpec(memory_space=pl.ANY)
    basis, codes = pl.pallas_call(
        functools.partial(kernel, clus, help_, cap),
        out_shape=(
            jax.ShapeDtypeStruct((rank, share), F32),
            jax.ShapeDtypeStruct((stored, rank, block_rows), BF16),
        ),
        in_specs=[smem, smem, vmem, hbm, hbm, hbm],
        out_specs=(vmem, vmem),
        scratch_shapes=[
            pltpu.VMEM((clus * help_, share, depth), BF16),
            pltpu.VMEM((stored, block_rows, depth), BF16),
            pltpu.VMEM((clus * cap, block_rows, depth), BF16),
            pltpu.VMEM((clus * cap, block_rows, queries_all), BF16),
            pltpu.VMEM((POWER + 1, clus * rank, queries_all), BF16),
            pltpu.VMEM((clus * rank, queries_all), F32),
            pltpu.VMEM((clus, rank, queries_all), F32),
            pltpu.VMEM((POWER, rank, queries_all), F32),
            pltpu.VMEM((POWER, help_, rank, share), F32),
            pltpu.VMEM((POWER, help_, rank, 128), F32),
            dma((3,)),
            dma((2, help_)), dma((help_,)),
            dma((nx, help_)), dma((nx, help_)),
            dma((nx, help_)), dma((nx, help_)),
            dma((POWER + 1, help_)), dma((POWER + 1, help_)),
            dma((POWER + 1, clus)), dma((POWER + 1, clus)),
            dma((POWER, clus)), dma((POWER, clus)),
            dma((POWER, help_)), dma((POWER, help_)),
            dma((POWER, help_)), dma((POWER, help_)),
        ],
        compiler_params=pltpu.CompilerParams(
            collective_id=0, has_side_effects=True, vmem_limit_bytes=62 * 1024 * 1024
        ),
    )(source, slot, owner_wide, item_row_blocks, query_rows[0], sketch_rows[0])
    return (basis[None], codes)


def solution(mesh):
    in_specs = (
        P(("groups", "clus", "help"), None, None),
        P(("groups", "clus", "help"), None),
        P("groups"),
        P(("groups", "clus"), "help", None),
        P(("groups", "clus"), None, "help"),
    )
    out_specs = (P(("groups", "clus"), None, "help"), P(("groups", "clus", "help"), None, None))
    return jax.shard_map(
        on_device, mesh=mesh, in_specs=in_specs, out_specs=out_specs, check_vma=False
    )
```

time: 276 us -> 125 us (0.45)
  waiting for transfers between devices: 154 us -> 0 us
  Pallas kernels: 0 us -> 119 us
  matrix products: 56.4 us -> 0 us
  blocking collectives: 15 us -> 0 us
  between operations: 13.8 us -> 0.65 us
  other arithmetic: 14.3 us -> 1.54 us
  starting transfers between devices: 9.57 us -> 0 us
  local copies, waits for them, and re-layouts: 12.8 us -> 3.7 us
    pallas_call x0 -> x1, Pallas kernels: none -> 119 us  [on_device(): pl.pallas_call(functools.partial(kernel, clus, help_, cap), out_shape=(ja...]
    psum x2 -> x0, waiting for transfers between devices: 69.8 us -> none  [on_device(): summed = lax.psum(partial_value, 'help')]
    dot_general x8 -> x0, matrix products: 53.9 us -> none  [the longest x2 20.9 us: on_device(): jnp.einsum('srk,smk->rm', codes_now, scores, preferred_element_type=jnp.f...]
    all_to_all x2 -> x0, waiting for transfers between devices: 47.5 us -> none  [the longest x1 42.2 us: on_device(): lax.all_to_all(packed, 'clus', split_axis=0, concat_axis=0, tiled=True)]
    all_gather x1 -> x0, waiting for transfers between devices: 35.8 us -> none  [on_device(): lax.all_gather(query_rows, 'help', axis=1, tiled=True)]
    all_gather x1 -> x0, blocking collectives: 15 us -> none  [on_device(): lax.all_gather(sketch_rows, 'help', axis=2, tiled=True)]
    another operation x10 -> x0, other arithmetic: 13.4 us -> none  [the longest x6 7.19 us: orthonormal(): factor_lower = jnp.linalg.cholesky(gram_matrix)]
    reshape x1 -> x0, local copies, waits for them, and re-layouts: 11.4 us -> none  [on_device(): packed = packed.reshape(clus_count, capacity, block_rows, depth)]
  transfers between devices with their start and end apart: 5 -> 0, of which waited for: 5 -> 0; matrix products, arithmetic and copies ran while one was open for 0% -> 0% of each run, Pallas kernels for 0% -> 0%
where the time goes in v1:
time: 125 us
  Pallas kernels  119 us (95%)
  local copies, waits for them, and re-layouts  3.7 us (3%)
  other arithmetic  1.54 us (1%)
    pallas_call x1, Pallas kernels, on_device(): pl.pallas_call(functools.partial(kernel, clus, help_, cap), out_shape=(ja...  119 us
    unnamed x4, local copies, waits for them, and re-layouts  2.95 us

profile of v1, /device:TPU:0, one launch (start us, length us, event | category | flops | bytes accessed | tf_op | source)
XLA Modules:
  0.0 124.8 jit_solution(13549584856283656728)
XLA Ops:
  0.6 0.8 select_reduce_fusion.1
  1.4 0.2 convert_reduce_fusion
  1.6 0.0 copy-start
  1.6 0.6 select_reduce_fusion.src_ref
  2.2 0.1 broadcast_in_dim.47
  2.3 0.7 broadcast_in_dim.48
  2.9 0.0 copy-done
  2.9 119.0 %shard_map.68 = (f32[32,256]{1,0:T(8,128)}, bf16[16,32,128]{2,1,0:T(8,128)(2,1)}) custom-call(s32[32]{0:T(128)} %select_reduce_fusion.src_ref, s32[16]{0:T(128)} %copy-done, s32[4,1,512]{2,1,0:T(1,128)} %bitcast.6, bf16[16,128,1024]{2,1,0:T(8,128)(2,1)} %item_ref.1, bf16[256,1024]{1,0:T(8,128)(2,1)} %bitcast.5, bf16[32,256]{1,0:T(8,128)(2,1)} %bitcast.8), custom_call_target="tpu_custom_call" | custom-call | tf_op jit(solution)/shard_map/pallas_call | solution.py:367
  121.9 1.4 %copy.9 = f32[1,32,256]{2,1,0:T(8,128)} copy(f32[1,32,256]{2,1,0:T(8,128)} %bitcast.7) | data formatting | bytes 65536
  123.3 1.6 %copy.10 = bf16[16,32,128]{2,1,0:T(8,128)(2,1)} copy(bf16[16,32,128]{2,1,0:T(8,128)(2,1)} %get-tuple-element.9) | data formatting | bytes 262144
  (1 shorter events, 0.0 us)
Async XLA Ops:
  1.6 1.4 %copy-start = (s32[16]{0:T(128)}, s32[16]{0:T(128)S(1)}, u32[]{:S(2)}) copy-start(s32[16]{0:T(128)S(1)} %multiply_add_fusion.slot_ref) | copy-start | bytes 196

commit v2 on v1

--- a/solution.py
+++ b/solution.py
@@ -144,29 +144,33 @@
             c, lax.rem(h + k, help_),
         )
 
-    def gx(stage, k):
+    def gx(stage, k, j):
         return remote(
-            left.at[stage, own_rows], gxs.at[stage, k], gxr.at[stage, k],
+            left.at[stage, own_rows, cols(j)], gxs.at[stage, k, j], gxr.at[stage, k, j],
             lax.rem(c + k, clus), h,
         )
 
     def gather_first(stage):
         for k in range(1, help_):
             gz(stage, k).start()
+        for k in range(1, clus):
+            gx(stage, k, h).start()
 
     def gather_second(stage):
-        for k in range(1, help_):
-            gz(stage, k).wait_recv()
-        for k in range(1, clus):
-            gx(stage, k).start()
+        for kz in range(1, help_):
+            gz(stage, kz).wait_recv()
+            for k in range(1, clus):
+                gx(stage, k, lax.rem(h + help_ - kz, help_)).start()
 
     def gather_finish(stage):
         for k in range(1, clus):
-            gx(stage, k).wait_recv()
+            for j in range(help_):
+                gx(stage, k, j).wait_recv()
         for k in range(1, help_):
             gz(stage, k).wait_send()
         for k in range(1, clus):
-            gx(stage, k).wait_send()
+            for j in range(help_):
+                gx(stage, k, j).wait_send()
 
     load_query.wait()
     spread(0)
@@ -233,20 +237,27 @@
 
     group = 4
     width = group * block_rows
-    row_owner = lax.broadcasted_iota(jnp.int32, (clus * rank, width), 0) // rank
+    row_owner = lax.broadcasted_iota(jnp.int32, (clus * rank, block_rows), 0) // rank
 
     def make_codes(stage, g):
         part = scores[pl.ds(g * group, group)].reshape(width, left.shape[2])
         value = dot_nt(left[stage], part)
-        keep = row_owner == owner_ref[g]
-        return jnp.where(keep, value, 0.0), part
-
-    def a_copy(it, k):
+        kept = [
+            jnp.where(
+                row_owner == owner_ref[g * group + b],
+                value[:, b * block_rows : (b + 1) * block_rows],
+                0.0,
+            )
+            for b in range(group)
+        ]
+        return jnp.concatenate(kept, axis=1), part
+
+    def a_copy(it, k, j):
         to = lax.rem(c + k, clus)
         return pltpu.make_async_remote_copy(
-            src_ref=partial.at[pl.ds(pl.multiple_of(to * rank, rank), rank)],
-            dst_ref=from_clus.at[k],
-            send_sem=as_.at[it, k], recv_sem=ar.at[it, k],
+            src_ref=partial.at[pl.ds(pl.multiple_of(to * rank, rank), rank), cols(j)],
+            dst_ref=from_clus.at[k, :, cols(j)],
+            send_sem=as_.at[it, k, j], recv_sem=ar.at[it, k, j],
             device_id=at(to, h), device_id_type=MESH,
         )
 
@@ -271,16 +282,18 @@
                 partial[...] = term
             else:
                 partial[...] += term
-        for k in range(1, clus):
-            a_copy(it, k).start()
-        summed = partial[own_rows]
-        for k in range(1, clus):
-            a_copy(it, k).wait_recv()
-            summed = summed + from_clus[k]
-        total[it] = summed
-        for k in range(1, help_):
-            b_copy(it, k).start()
-        mine = total[it, :, cols(h)]
+        for kz in range(1, help_ + 1):
+            for k in range(1, clus):
+                a_copy(it, k, lax.rem(h + kz, help_)).start()
+        for kz in range(1, help_ + 1):
+            j = lax.rem(h + kz, help_)
+            mine = partial[own_rows, cols(j)]
+            for k in range(1, clus):
+                a_copy(it, k, j).wait_recv()
+                mine = mine + from_clus[k, :, cols(j)]
+            if kz < help_:
+                total[it, :, cols(j)] = mine
+                b_copy(it, kz).start()
         for k in range(1, help_):
             b_copy(it, k).wait_recv()
             mine = mine + from_help[it, k]
@@ -303,7 +316,8 @@
             basis_ref[...] = basis
         gather_second(it + 1)
         for k in range(1, clus):
-            a_copy(it, k).wait_send()
+            for j in range(help_):
+                a_copy(it, k, j).wait_send()
         for k in range(1, help_):
             b_copy(it, k).wait_send()
             m_copy(it, k).wait_send()
@@ -357,7 +371,6 @@
     slot = owner * cap + jnp.sum(earlier.astype(jnp.int32), axis=1)
     every_slot = jnp.arange(clus * cap, dtype=jnp.int32)
     source = jnp.sum(jnp.where(every_slot[:, None] == slot[None, :], order[None, :], 0), axis=1)
-    owner_wide = jnp.repeat(owner, block_rows).reshape(stored // 4, 1, 4 * block_rows)
 
     nx = clus // CORES
     dma = pltpu.SemaphoreType.DMA
@@ -370,7 +383,7 @@
             jax.ShapeDtypeStruct((rank, share), F32),
             jax.ShapeDtypeStruct((stored, rank, block_rows), BF16),
         ),
-        in_specs=[smem, smem, vmem, hbm, hbm, hbm],
+        in_specs=[smem, smem, smem, hbm, hbm, hbm],
         out_specs=(vmem, vmem),
         scratch_shapes=[
             pltpu.VMEM((clus * help_, share, depth), BF16),
@@ -388,15 +401,15 @@
             dma((nx, help_)), dma((nx, help_)),
             dma((nx, help_)), dma((nx, help_)),
             dma((POWER + 1, help_)), dma((POWER + 1, help_)),
-            dma((POWER + 1, clus)), dma((POWER + 1, clus)),
-            dma((POWER, clus)), dma((POWER, clus)),
+            dma((POWER + 1, clus, help_)), dma((POWER + 1, clus, help_)),
+            dma((POWER, clus, help_)), dma((POWER, clus, help_)),
             dma((POWER, help_)), dma((POWER, help_)),
             dma((POWER, help_)), dma((POWER, help_)),
         ],
         compiler_params=pltpu.CompilerParams(
             collective_id=0, has_side_effects=True, vmem_limit_bytes=62 * 1024 * 1024
         ),
-    )(source, slot, owner_wide, item_row_blocks, query_rows[0], sketch_rows[0])
+    )(source, slot, owner, item_row_blocks, query_rows[0], sketch_rows[0])
     return (basis[None], codes)
 
 

time: 125 us -> 122 us (0.976)
  Pallas kernels: 119 us -> 117 us
    pallas_call x1, Pallas kernels: 119 us -> 117 us  [on_device(): pl.pallas_call(functools.partial(kernel, clus, help_, cap), out_shape=(ja...]
    unnamed x4 -> x6, local copies, waits for them, and re-layouts: 2.95 us -> 2.95 us
where the time goes in v2:
time: 122 us
  Pallas kernels  117 us (96%)
  local copies, waits for them, and re-layouts  2.95 us (2%)
  other arithmetic  1.54 us (1%)
    pallas_call x1, Pallas kernels, on_device(): pl.pallas_call(functools.partial(kernel, clus, help_, cap), out_shape=(ja...  117 us
    unnamed x6, local copies, waits for them, and re-layouts  2.95 us

profile of v2, /device:TPU:0, one launch (start us, length us, event | category | flops | bytes accessed | tf_op | source)
XLA Modules:
  0.0 122.0 jit_solution(16222692321489740659)
XLA Ops:
  0.6 0.8 select_reduce_fusion.1.owner_ref
  1.4 0.0 copy-start
  1.4 0.2 convert_reduce_fusion
  1.6 0.0 copy-start.1
  1.6 0.6 select_reduce_fusion.src_ref
  2.2 0.0 copy-done
  2.2 0.0 copy-done.1
  2.2 116.8 %shard_map.68 = (f32[32,256]{1,0:T(8,128)}, bf16[16,32,128]{2,1,0:T(8,128)(2,1)}) custom-call(s32[32]{0:T(128)} %select_reduce_fusion.src_ref, s32[16]{0:T(128)} %copy-done.1, s32[16]{0:T(128)} %copy-done, bf16[16,128,1024]{2,1,0:T(8,128)(2,1)} %item_ref.1, bf16[256,1024]{1,0:T(8,128)(2,1)} %bitcast.4, bf16[32,256]{1,0:T(8,128)(2,1)} %bitcast.6), custom_call_target="tpu_custom_call" | custom-call | tf_op jit(solution)/shard_map/pallas_call | solution.py:380
  119.0 1.4 %copy.9 = f32[1,32,256]{2,1,0:T(8,128)} copy(f32[1,32,256]{2,1,0:T(8,128)} %bitcast.5) | data formatting | bytes 65536
  120.4 1.6 %copy.10 = bf16[16,32,128]{2,1,0:T(8,128)(2,1)} copy(bf16[16,32,128]{2,1,0:T(8,128)(2,1)} %get-tuple-element.9) | data formatting | bytes 262144
  (1 shorter events, 0.0 us)
Async XLA Ops:
  1.4 0.8 copy-start
  1.6 0.6 copy-start.1

commit v3 on v2

--- a/solution.py
+++ b/solution.py
@@ -9,6 +9,7 @@
 
 POWER = 2
 CORES = 2
+HALVES = 2
 MESH = pl.DeviceIdType.MESH
 F32 = jnp.float32
 BF16 = jnp.bfloat16
@@ -41,7 +42,7 @@
     src_ref, slot_ref, owner_ref, item_ref, query_ref, sketch_ref,
     basis_ref, codes_ref,
     queries, items, packed, slots, left, partial, from_clus, total, from_help, grams,
-    load_sem, zs, zr, xs, xr, cs, cr, gzs, gzr, gxs, gxr, as_, ar, bs, br, ms, mr,
+    load_sem, zs, zr, xs, xr, cs, cr, es, er, gzs, gzr, gxs, gxr, as_, ar, bs, br, ms, mr,
 ):
     nx = clus // CORES
     stored, block_rows, depth = items.shape
@@ -87,16 +88,34 @@
             device_id=at(ci, hi), device_id_type=MESH,
         )
 
-    def z_copy(d, j):
+    half = share // HALVES
+    partner = h + 1 - 2 * (h % 2)
+
+    def piece(ci, j, q):
+        return queries.at[ci * help_ + j, pl.ds(q * half, half)]
+
+    def z_copy(d, j, q):
         hi = jnp.clip(h + 1 if d == 0 else h - 1, 0, help_ - 1)
-        return remote(queries.at[c * help_ + j], zs.at[d, j], zr.at[j], c, hi)
-
-    def x_copy(ci, dx, j):
+        return remote(piece(c, j, q), zs.at[d, j, q], zr.at[j, q], c, hi)
+
+    def x_copy(ci, dx, j, q):
         other = lax.rem(x + dx, nx) * CORES + core
-        return remote(queries.at[ci * help_ + j], xs.at[dx, j], xr.at[dx, j], other, h)
-
-    def core_copy(ci, dx, j):
-        return remote(queries.at[ci * help_ + j], cs.at[dx, j], cr.at[dx, j], sib, h)
+        return remote(piece(ci, j, q), xs.at[dx, j, q], xr.at[dx, j, q], other, h)
+
+    def core_copy(ci, dx, j, q):
+        return remote(piece(ci, j, q), cs.at[dx, j, q], cr.at[dx, j, q], sib, h)
+
+    def late_copy(ci, dx, j):
+        return remote(piece(ci, j, HALVES - 1), es.at[dx], er.at[dx], c, partner)
+
+    def x_source(dx):
+        return lax.rem(x + nx - dx, nx) * CORES + core
+
+    def unless_late(j, q, action):
+        if q < HALVES - 1:
+            action()
+        else:
+            pl.when(j != partner)(action)
 
     def slice_of(s, d):
         j = jnp.where(d == 0, h - s, h + s)
@@ -109,22 +128,26 @@
 
             @pl.when(ok)
             def _():
-                if not (isinstance(s, int) and s == 0):
-                    z_copy(d, j).wait_recv()
-
-                @pl.when(h < help_ - 1 if d == 0 else h > 0)
-                def _():
-                    z_copy(d, j).start()
-
-                if isinstance(s, int) and s == 0 and d == 0:
-
-                    @pl.when(h > 0)
+                for q in range(HALVES):
+                    if not (isinstance(s, int) and s == 0):
+                        z_copy(d, j, q).wait_recv()
+
+                    @pl.when(h < help_ - 1 if d == 0 else h > 0)
                     def _():
-                        z_copy(1, j).start()
-
-                for dx in range(1, nx):
-                    x_copy(c, dx, j).start()
-                core_copy(c, 0, j).start()
+                        z_copy(d, j, q).start()
+
+                    if isinstance(s, int) and s == 0 and d == 0:
+
+                        @pl.when(h > 0)
+                        def _():
+                            z_copy(1, j, q).start()
+
+                    def to_x():
+                        for dx in range(1, nx):
+                            x_copy(c, dx, j, q).start()
+
+                    unless_late(j, q, to_x)
+                    core_copy(c, 0, j, q).start()
 
     group_rows = min(4, cap)
 
@@ -186,6 +209,11 @@
 
     @pl.loop(0, help_ + 2)
     def _(s):
+        @pl.when(s == help_ - 1)
+        def _():
+            for dx in range(1, nx):
+                late_copy(x_source(dx), dx, h).start()
+
         @pl.when((s > 0) & (s < help_))
         def _():
             spread(s)
@@ -201,33 +229,55 @@
         @pl.loop(0, 2)
         def _(d):
             j, ok = slice_of(s - 1, d)
+
+            @pl.when(ok)
+            def _():
+                for q in range(HALVES):
+
+                    def pass_on():
+                        @pl.loop(1, nx)
+                        def _(dx):
+                            x_copy(x_source(dx), dx, j, q).wait_recv()
+                            core_copy(x_source(dx), dx, j, q).start()
+
+                    unless_late(j, q, pass_on)
+                    core_copy(sib, 0, j, q).wait_recv()
+
+                score(sib, j)
+
+                @pl.when(j != partner)
+                def _():
+                    @pl.loop(1, nx)
+                    def _(dx):
+                        score(x_source(dx), j)
+
+        @pl.loop(0, 2)
+        def _(d):
+            j, ok = slice_of(s - 2, d)
 
             @pl.when(ok)
             def _():
                 @pl.loop(1, nx)
                 def _(dx):
-                    ci = lax.rem(x + nx - dx, nx) * CORES + core
-                    x_copy(ci, dx, j).wait_recv()
-                    core_copy(ci, dx, j).start()
-
-                core_copy(sib, 0, j).wait_recv()
-                score(sib, j)
-
-                @pl.loop(1, nx)
-                def _(dx):
-                    score(lax.rem(x + nx - dx, nx) * CORES + core, j)
-
-        @pl.loop(0, 2)
-        def _(d):
-            j, ok = slice_of(s - 2, d)
-
-            @pl.when(ok)
-            def _():
-                @pl.loop(1, nx)
-                def _(dx):
-                    ci = lax.rem(x + nx - dx, nx) * CORES + (1 - core)
-                    core_copy(ci, dx, j).wait_recv()
-                    score(ci, j)
+                    ci = x_source(dx) + 1 - 2 * core
+                    for q in range(HALVES):
+                        unless_late(j, q, core_copy(ci, dx, j, q).wait_recv)
+
+                    @pl.when(j != partner)
+                    def _():
+                        score(ci, j)
+
+    @pl.loop(1, nx)
+    def _(dx):
+        late_copy(x_source(dx), dx, partner).wait_recv()
+        core_copy(x_source(dx), dx, partner, HALVES - 1).start()
+        score(x_source(dx), partner)
+
+    @pl.loop(1, nx)
+    def _(dx):
+        ci = x_source(dx) + 1 - 2 * core
+        core_copy(ci, dx, partner, HALVES - 1).wait_recv()
+        score(ci, partner)
 
     scores = items
 
@@ -339,20 +389,28 @@
 
             @pl.when(ok)
             def _():
-                @pl.when(h < help_ - 1 if d == 0 else h > 0)
-                def _():
-                    z_copy(d, j).wait_send()
-
-                if d == 0:
-
-                    @pl.when((s == 0) & (h > 0))
+                for q in range(HALVES):
+
+                    @pl.when(h < help_ - 1 if d == 0 else h > 0)
                     def _():
-                        z_copy(1, j).wait_send()
-
-                core_copy(c, 0, j).wait_send()
-                for dx in range(1, nx):
-                    x_copy(c, dx, j).wait_send()
-                    core_copy(c, dx, j).wait_send()
+                        z_copy(d, j, q).wait_send()
+
+                    if d == 0:
+
+                        @pl.when((s == 0) & (h > 0))
+                        def _():
+                            z_copy(1, j, q).wait_send()
+
+                    def sent_x():
+                        for dx in range(1, nx):
+                            x_copy(c, dx, j, q).wait_send()
+
+                    unless_late(j, q, sent_x)
+                    for dx in range(nx):
+                        core_copy(c, dx, j, q).wait_send()
+
+    for dx in range(1, nx):
+        late_copy(c, dx, h).wait_send()
 
 
 def on_device(item_row_blocks, block_cluster, cluster_owner, query_rows, sketch_rows):
@@ -397,9 +455,10 @@
             pltpu.VMEM((POWER, help_, rank, share), F32),
             pltpu.VMEM((POWER, help_, rank, 128), F32),
             dma((3,)),
-            dma((2, help_)), dma((help_,)),
-            dma((nx, help_)), dma((nx, help_)),
-            dma((nx, help_)), dma((nx, help_)),
+            dma((2, help_, HALVES)), dma((help_, HALVES)),
+            dma((nx, help_, HALVES)), dma((nx, help_, HALVES)),
+            dma((nx, help_, HALVES)), dma((nx, help_, HALVES)),
+            dma((nx,)), dma((nx,)),
             dma((POWER + 1, help_)), dma((POWER + 1, help_)),
             dma((POWER + 1, clus, help_)), dma((POWER + 1, clus, help_)),
             dma((POWER, clus, help_)), dma((POWER, clus, help_)),

time: 122 us -> 120 us (0.984)
  Pallas kernels: 117 us -> 114 us
    pallas_call x1, Pallas kernels: 117 us -> 114 us  [on_device(): pl.pallas_call(functools.partial(kernel, clus, help_, cap), out_shape=(ja...]
where the time goes in v3:
time: 120 us; the launch traced here: 119 us
  Pallas kernels  114 us (95%)
  local copies, waits for them, and re-layouts  2.95 us (2%)
  other arithmetic  1.54 us (1%)
    pallas_call x1, Pallas kernels, on_device(): pl.pallas_call(functools.partial(kernel, clus, help_, cap), out_shape=(ja...  114 us
    unnamed x6, local copies, waits for them, and re-layouts  2.95 us

profile of v3, /device:TPU:0, one launch (start us, length us, event | category | flops | bytes accessed | tf_op | source)
XLA Modules:
  0.0 119.3 jit_solution(15265773119783793909)
XLA Ops:
  0.6 0.8 select_reduce_fusion.1.owner_ref
  1.4 0.0 copy-start
  1.4 0.2 convert_reduce_fusion
  1.6 0.0 copy-start.1
  1.6 0.6 select_reduce_fusion.src_ref
  2.2 0.0 copy-done
  2.2 0.0 copy-done.1
  2.2 114.2 %shard_map.68 = (f32[32,256]{1,0:T(8,128)}, bf16[16,32,128]{2,1,0:T(8,128)(2,1)}) custom-call(s32[32]{0:T(128)} %select_reduce_fusion.src_ref, s32[16]{0:T(128)} %copy-done.1, s32[16]{0:T(128)} %copy-done, bf16[16,128,1024]{2,1,0:T(8,128)(2,1)} %item_ref.1, bf16[256,1024]{1,0:T(8,128)(2,1)} %bitcast.4, bf16[32,256]{1,0:T(8,128)(2,1)} %bitcast.6), custom_call_target="tpu_custom_call" | custom-call | tf_op jit(solution)/shard_map/pallas_call | solution.py:438
  116.4 1.4 %copy.9 = f32[1,32,256]{2,1,0:T(8,128)} copy(f32[1,32,256]{2,1,0:T(8,128)} %bitcast.5) | data formatting | bytes 65536
  117.8 1.6 %copy.10 = bf16[16,32,128]{2,1,0:T(8,128)(2,1)} copy(bf16[16,32,128]{2,1,0:T(8,128)(2,1)} %get-tuple-element.9) | data formatting | bytes 262144
  (1 shorter events, 0.0 us)
Async XLA Ops:
  1.4 0.8 copy-start
  1.6 0.6 copy-start.1

commit v4 on v3

--- a/solution.py
+++ b/solution.py
@@ -41,7 +41,7 @@
     clus, help_, cap,
     src_ref, slot_ref, owner_ref, item_ref, query_ref, sketch_ref,
     basis_ref, codes_ref,
-    queries, items, packed, slots, left, partial, from_clus, total, from_help, grams,
+    queries, items, packed, slots, left, partial, from_clus, early_clus, total, from_help, grams,
     load_sem, zs, zr, xs, xr, cs, cr, es, er, gzs, gzr, gxs, gxr, as_, ar, bs, br, ms, mr,
 ):
     nx = clus // CORES
@@ -304,6 +304,15 @@
 
     def a_copy(it, k, j):
         to = lax.rem(c + k, clus)
+        if it < POWER - 1:
+            slot_of = to // (block_rows // rank)
+            row = pl.ds(pl.multiple_of(to % (block_rows // rank) * rank, rank), rank)
+            return pltpu.make_async_remote_copy(
+                src_ref=packed.at[slot_of, row, cols(j)],
+                dst_ref=early_clus.at[k, :, cols(j)],
+                send_sem=as_.at[it, k, j], recv_sem=ar.at[it, k, j],
+                device_id=at(to, h), device_id_type=MESH,
+            )
         return pltpu.make_async_remote_copy(
             src_ref=partial.at[pl.ds(pl.multiple_of(to * rank, rank), rank), cols(j)],
             dst_ref=from_clus.at[k, :, cols(j)],
@@ -332,6 +341,9 @@
                 partial[...] = term
             else:
                 partial[...] += term
+        if it < POWER - 1:
+            for n in range(clus * rank // block_rows):
+                packed[n] = partial[n * block_rows : (n + 1) * block_rows].astype(BF16)
         for kz in range(1, help_ + 1):
             for k in range(1, clus):
                 a_copy(it, k, lax.rem(h + kz, help_)).start()
@@ -340,7 +352,8 @@
             mine = partial[own_rows, cols(j)]
             for k in range(1, clus):
                 a_copy(it, k, j).wait_recv()
-                mine = mine + from_clus[k, :, cols(j)]
+                got = early_clus if it < POWER - 1 else from_clus
+                mine = mine + got[k, :, cols(j)].astype(F32)
             if kz < help_:
                 total[it, :, cols(j)] = mine
                 b_copy(it, kz).start()
@@ -451,6 +464,7 @@
             pltpu.VMEM((POWER + 1, clus * rank, queries_all), BF16),
             pltpu.VMEM((clus * rank, queries_all), F32),
             pltpu.VMEM((clus, rank, queries_all), F32),
+            pltpu.VMEM((clus, rank, queries_all), BF16),
             pltpu.VMEM((POWER, rank, queries_all), F32),
             pltpu.VMEM((POWER, help_, rank, share), F32),
             pltpu.VMEM((POWER, help_, rank, 128), F32),
@@ -466,7 +480,7 @@
             dma((POWER, help_)), dma((POWER, help_)),
         ],
         compiler_params=pltpu.CompilerParams(
-            collective_id=0, has_side_effects=True, vmem_limit_bytes=62 * 1024 * 1024
+            collective_id=0, has_side_effects=True, vmem_limit_bytes=63 * 1024 * 1024
         ),
     )(source, slot, owner, item_row_blocks, query_rows[0], sketch_rows[0])
     return (basis[None], codes)

time: 120 us -> 118 us (0.983)
    pallas_call x1, Pallas kernels: 114 us -> 113 us  [on_device(): pl.pallas_call(functools.partial(kernel, clus, help_, cap), out_shape=(ja...]
where the time goes in v4:
time: 118 us
  Pallas kernels  113 us (96%)
  local copies, waits for them, and re-layouts  2.95 us (2%)
  other arithmetic  1.54 us (1%)
    pallas_call x1, Pallas kernels, on_device(): pl.pallas_call(functools.partial(kernel, clus, help_, cap), out_shape=(ja...  113 us
    unnamed x6, local copies, waits for them, and re-layouts  2.95 us

profile of v4, /device:TPU:0, one launch (start us, length us, event | category | flops | bytes accessed | tf_op | source)
XLA Modules:
  0.0 118.0 jit_solution(11474799428257182732)
XLA Ops:
  0.6 0.8 select_reduce_fusion.1.owner_ref
  1.4 0.0 copy-start
  1.4 0.2 convert_reduce_fusion
  1.6 0.0 copy-start.1
  1.6 0.6 select_reduce_fusion.src_ref
  2.2 0.0 copy-done
  2.2 0.0 copy-done.1
  2.2 112.9 %shard_map.68 = (f32[32,256]{1,0:T(8,128)}, bf16[16,32,128]{2,1,0:T(8,128)(2,1)}) custom-call(s32[32]{0:T(128)} %select_reduce_fusion.src_ref, s32[16]{0:T(128)} %copy-done.1, s32[16]{0:T(128)} %copy-done, bf16[16,128,1024]{2,1,0:T(8,128)(2,1)} %item_ref.1, bf16[256,1024]{1,0:T(8,128)(2,1)} %bitcast.4, bf16[32,256]{1,0:T(8,128)(2,1)} %bitcast.6), custom_call_target="tpu_custom_call" | custom-call | tf_op jit(solution)/shard_map/pallas_call | solution.py:451
  115.1 1.4 %copy.9 = f32[1,32,256]{2,1,0:T(8,128)} copy(f32[1,32,256]{2,1,0:T(8,128)} %bitcast.5) | data formatting | bytes 65536
  116.5 1.6 %copy.10 = bf16[16,32,128]{2,1,0:T(8,128)(2,1)} copy(bf16[16,32,128]{2,1,0:T(8,128)(2,1)} %get-tuple-element.9) | data formatting | bytes 262144
  (1 shorter events, 0.0 us)
Async XLA Ops:
  1.4 0.8 copy-start
  1.6 0.6 copy-start.1
